TPU v7x, 32 devices: a whole 2x2x4 slice. The times are simulated.
32 devices in a mesh: shard: 4 (over z), rep: 8 (over y, x, core).
Axes of the slice: x: 2, y: 2, z: 4, core: 2. Of those that a mesh axis runs over, the one named last changes fastest.
Arguments:
- tokens: bfloat16 [128, 256, 384], P(('shard', 'rep')), may hold values from -6 to 6
- condition: bfloat16 [128, 384], P(('shard', 'rep')), may hold values from -6 to 6
- cotangent: bfloat16 [128, 256, 384], P(('shard', 'rep')), may hold values from -6 to 6
- attend_weight: float32 [384, 1152], P(None, 'shard'), may hold values from -0.3125 to 0.3125
- project_weight: float32 [384, 384], P(None, 'shard'), may hold values from -1.75 to 1.75
- expand_weight: float32 [384, 1536], P(None, 'shard'), may hold values from -0.3125 to 0.3125
- contract_weight: float32 [384, 1536], P(None, 'shard'), may hold values from -0.15625 to 0.15625
- modulate_weight: float32 [384, 2304], P(None, 'shard'), may hold values from -0.3125 to 0.3125
- biases: float32 [4224], P('shard'), may hold values from -1.2 to 1.2
- attend_moment: float32 [384, 1152], P(None, 'shard'), may hold values from -2606.6784 to 2606.6784
- project_moment: float32 [384, 384], P(None, 'shard'), may hold values from -488.7522 to 488.7522
- expand_moment: float32 [384, 1536], P(None, 'shard'), may hold values from -814.58701 to 814.58701
- contract_moment: float32 [384, 1536], P(None, 'shard'), may hold values from -1629.17402 to 1629.17402
- modulate_moment: float32 [384, 2304], P(None, 'shard'), may hold values from -1955.0088 to 1955.0088
- bias_first: float32 [4224], P('shard'), may hold values from -121.282955 to 121.282955
- bias_second: float32 [4224], P('shard'), may hold values from 0.65536 to 262.144, as said below
Outputs:
- block_output: bfloat16 [128, 256, 384], P(('shard', 'rep'))
- tokens_grad: float32 [128, 256, 384], P(('shard', 'rep'))
- condition_grad: float32 [128, 384], P(('shard', 'rep'))
- attend_grad: float32 [384, 1152], P(None, 'shard')
- project_grad: float32 [384, 384], P(None, 'shard')
- expand_grad: float32 [384, 1536], P(None, 'shard')
- contract_grad: float32 [384, 1536], P(None, 'shard')
- modulate_grad: float32 [384, 2304], P(None, 'shard')
- attend_momentum: float32 [384, 1152], P(None, 'shard')
- project_momentum: float32 [384, 384], P(None, 'shard')
- expand_momentum: float32 [384, 1536], P(None, 'shard')
- contract_momentum: float32 [384, 1536], P(None, 'shard')
- modulate_momentum: float32 [384, 2304], P(None, 'shard')
- attend_updated: float32 [384, 1152], P(None, 'shard')
- project_updated: float32 [384, 384], P(None, 'shard')
- expand_updated: float32 [384, 1536], P(None, 'shard')
- contract_updated: float32 [384, 1536], P(None, 'shard')
- modulate_updated: float32 [384, 2304], P(None, 'shard')
- bias_gradient: float32 [4224], P('shard')
- bias_momentum: float32 [4224], P('shard')
- bias_variance: float32 [4224], P('shard')
- bias_updated: float32 [4224], P('shard')
Inputs may be any that keep to these rules, and one draw needn't show every extreme that they name: `bias_second`: second moment of the biases, positive.
All inputs are finite; a program needn't handle non-finite values.
Results may differ from a plain program's by a relative error of at most 0.013.
The roundings to bfloat16 on the way count: a program that leaves them out, or rounds other values in their place, can miss the bound.
Values may be sent and summed in bfloat16 or wider, within the bound.
No kernel may reach another device: no remote copies, remote signals or barrier semaphores. Data moves between devices by JAX's collectives and lax.ppermute only.
A program may use at most 128 MiB of HBM per device.

v0:
```python
from functools import partial
import math

import jax
import jax.numpy as jnp
from jax import lax
from jax.sharding import PartitionSpec as P

D = 384
HEADS = 6
HEAD = 64
FF = 1536
LEN = 256
NS_ITERS = 5
STEP = 10


EXACT_PRECISION = lax.Precision.HIGHEST
POLY_LINEAR = 3.4445
POLY_CUBIC = -4.775
POLY_QUINTIC = 2.0315
MOMENTUM = 0.95
MUON_RATE = 0.4
WEIGHT_DECAY = 0.01
ADAM_RATE = 0.1
BETA_ONE = 0.9
BETA_TWO = 0.999
ADAM_EPSILON = 1e-08


def normalize(values):
    centered = values - jnp.mean(values, -1, keepdims=True)
    inverse_spread = lax.rsqrt(jnp.mean(centered * centered, -1, keepdims=True) + 1e-06)
    return (centered * inverse_spread, inverse_spread)


def normalize_back(upstream, normed, inverse_spread):
    return inverse_spread * (
        upstream
        - jnp.mean(upstream, -1, keepdims=True)
        - normed * jnp.mean(upstream * normed, -1, keepdims=True)
    )


def poly_step(column_block, gram):
    mixing = POLY_CUBIC * gram + POLY_QUINTIC * jnp.dot(gram, gram, precision=EXACT_PRECISION)
    return POLY_LINEAR * column_block + jnp.dot(mixing, column_block, precision=EXACT_PRECISION)


def newton_schulz(matrix):
    current = matrix / (jnp.sqrt(jnp.sum(matrix * matrix)) + 1e-07)
    for iteration in range(NS_ITERS):
        gram = jnp.einsum("rc,dc->rd", current, current, precision=EXACT_PRECISION)
        current = poly_step(current, gram)
    return current


def pad_columns(blocks, width, rows):
    filled = sum((block.shape[1] for block in blocks))
    if filled < width:
        blocks = blocks + [jnp.zeros((rows, width - filled), jnp.float32)]
    return jnp.concatenate(blocks, axis=1)


def owner_orthogonalize(column_shares):
    devices = lax.axis_size("shard")
    widths = [share.shape[1] for share in column_shares]
    owned = [
        [number for number in range(len(column_shares)) if number % devices == owner]
        for owner in range(devices)
    ]
    offsets = {}
    for owner in range(devices):
        running = 0
        for number in owned[owner]:
            offsets[number] = running
            running = running + widths[number]
    slot_width = max((sum((widths[number] for number in members)) for members in owned))
    outgoing = jnp.stack(
        [
            pad_columns([column_shares[number] for number in owned[owner]], slot_width, D)
            for owner in range(devices)
        ],
        axis=0,
    )
    incoming = lax.all_to_all(outgoing, "shard", split_axis=0, concat_axis=0, tiled=True)

    def owner_work(owner):

        def run(received):
            results = []
            for number in owned[owner]:
                start = offsets[number]
                whole = jnp.concatenate(
                    [
                        received[source][:, start : start + widths[number]]
                        for source in range(devices)
                    ],
                    axis=1,
                )
                results.append(newton_schulz(whole))
            slots = []
            for source in range(devices):
                slots.append(
                    pad_columns(
                        [
                            result[:, source * widths[number] : (source + 1) * widths[number]]
                            for result, number in zip(results, owned[owner])
                        ],
                        slot_width,
                        D,
                    )
                )
            return jnp.stack(slots, axis=0)

        return run

    replies = lax.switch(
        lax.axis_index("shard"), [owner_work(owner) for owner in range(devices)], incoming
    )
    returned = lax.all_to_all(replies, "shard", split_axis=0, concat_axis=0, tiled=True)
    return [
        returned[number % devices][:, offsets[number] : offsets[number] + widths[number]]
        for number in range(len(column_shares))
    ]


def per_device(
    tokens,
    condition,
    cotangent,
    attend_weight,
    project_weight,
    expand_weight,
    contract_weight,
    modulate_weight,
    biases,
    attend_moment,
    project_moment,
    expand_moment,
    contract_moment,
    modulate_moment,
    bias_first,
    bias_second,
):
    bfloat = jnp.bfloat16
    single_layer_input = jnp.float32
    latents = tokens.shape[0]
    (
        attention_weight_whole,
        projection_weight_whole,
        widening_weight_whole,
        narrowing_weight_whole,
        modulate_full,
        bias_full,
    ) = (
        lax.all_gather(attend_weight.astype(bfloat), "shard", axis=1, tiled=True),
        lax.all_gather(project_weight.astype(bfloat), "shard", axis=1, tiled=True),
        lax.all_gather(expand_weight.astype(bfloat), "shard", axis=1, tiled=True),
        lax.all_gather(contract_weight.astype(bfloat), "shard", axis=1, tiled=True),
        lax.all_gather(modulate_weight.astype(bfloat), "shard", axis=1, tiled=True),
        lax.all_gather(biases.astype(bfloat), "shard", axis=0, tiled=True),
    )
    ada_bias = bias_full[: 6 * D].astype(single_layer_input)
    widening_bias = bias_full[6 * D : 6 * D + FF].astype(single_layer_input)
    narrowing_bias = bias_full[6 * D + FF :].astype(single_layer_input)
    inputs = tokens.astype(single_layer_input)
    silu_value, silu_back = jax.vjp(jax.nn.silu, condition.astype(single_layer_input))
    cond_low = silu_value.astype(bfloat)
    modulation = (
        jnp.dot(cond_low, modulate_full, preferred_element_type=single_layer_input) + ada_bias
    )
    shift_one, scale_one, gate_one, shift_two, scale_two, gate_two = jnp.split(
        modulation[:, None, :], 6, axis=2
    )
    normed_one, spread_one = normalize(inputs)
    residual_first = (normed_one * (1.0 + scale_one) + shift_one).astype(bfloat)
    projection_output = jnp.einsum(
        "rvx,xf->rvf",
        residual_first,
        attention_weight_whole,
        preferred_element_type=single_layer_input,
    ).astype(bfloat)
    heads_view = projection_output.reshape(latents, LEN, 3, HEADS, HEAD)
    queries = heads_view[:, :, 0]
    key_heads = heads_view[:, :, 1]
    value_heads = heads_view[:, :, 2]
    score_scale = HEAD ** (-0.5)
    scores = (
        jnp.einsum("sqhe,skhe->shqk", queries, key_heads, preferred_element_type=single_layer_input)
        * score_scale
    )
    log_total = jax.nn.logsumexp(scores, axis=-1, keepdims=True)
    attention_low = jnp.exp(scores - log_total).astype(bfloat)
    attention_output = (
        jnp.einsum(
            "shqk,skhe->sqhe", attention_low, value_heads, preferred_element_type=single_layer_input
        )
        .reshape(latents, LEN, D)
        .astype(bfloat)
    )
    attention_branch = jnp.einsum(
        "rvx,xf->rvf",
        attention_output,
        projection_weight_whole,
        preferred_element_type=single_layer_input,
    )
    mixed = inputs + gate_one * attention_branch
    normed_two, spread_two = normalize(mixed)
    residual_second = (normed_two * (1.0 + scale_two) + shift_two).astype(bfloat)
    preactivation_value = (
        jnp.einsum(
            "pvk,km->pvm",
            residual_second,
            widening_weight_whole,
            preferred_element_type=single_layer_input,
        )
        + widening_bias
    )
    act_value, act_back = jax.vjp(partial(jax.nn.gelu, approximate=True), preactivation_value)
    activation_reduced = act_value.astype(bfloat)
    perceptron_branch = (
        jnp.einsum(
            "mgr,ir->mgi",
            activation_reduced,
            narrowing_weight_whole,
            preferred_element_type=single_layer_input,
        )
        + narrowing_bias
    )
    block_output = (mixed + gate_two * perceptron_branch).astype(bfloat)
    grad_out = cotangent.astype(single_layer_input)
    grad_gate_two = jnp.sum(grad_out * perceptron_branch, axis=1, keepdims=True)
    branch_gradient = (gate_two * grad_out).astype(bfloat)
    narrowing_gradient = jnp.einsum(
        "gpr,gpw->rw",
        branch_gradient,
        activation_reduced,
        preferred_element_type=single_layer_input,
    )
    activation_gradient = jnp.einsum(
        "pvk,km->pvm",
        branch_gradient,
        narrowing_weight_whole,
        preferred_element_type=single_layer_input,
    )
    preactivation_gradient = act_back(activation_gradient)[0].astype(bfloat)
    widening_gradient = jnp.einsum(
        "gpr,gpw->rw",
        residual_second,
        preactivation_gradient,
        preferred_element_type=single_layer_input,
    )
    grad_hidden_two = jnp.einsum(
        "mgr,ir->mgi",
        preactivation_gradient,
        widening_weight_whole,
        preferred_element_type=single_layer_input,
    )
    grad_shift_two = jnp.sum(grad_hidden_two, axis=1, keepdims=True)
    grad_scale_two = jnp.sum(grad_hidden_two * normed_two, axis=1, keepdims=True)
    grad_mixed = grad_out + normalize_back(
        grad_hidden_two * (1.0 + scale_two), normed_two, spread_two
    )
    grad_gate_one = jnp.sum(grad_mixed * attention_branch, axis=1, keepdims=True)
    attention_branch_gradient = (gate_one * grad_mixed).astype(bfloat)
    grad_project = jnp.einsum(
        "ztm,ztg->mg",
        attention_output,
        attention_branch_gradient,
        preferred_element_type=single_layer_input,
    )
    grad_attended = (
        jnp.einsum(
            "hfc,zc->hfz",
            attention_branch_gradient,
            projection_weight_whole,
            preferred_element_type=single_layer_input,
        )
        .astype(bfloat)
        .reshape(latents, LEN, HEADS, HEAD)
    )
    scores_again = (
        jnp.einsum("sqhe,skhe->shqk", queries, key_heads, preferred_element_type=single_layer_input)
        * score_scale
    )
    attention = jnp.exp(scores_again - log_total)
    grad_attention = jnp.einsum(
        "sqhe,skhe->shqk", grad_attended, value_heads, preferred_element_type=single_layer_input
    )
    grad_scores = (
        attention * (grad_attention - jnp.sum(attention * grad_attention, axis=-1, keepdims=True))
    ).astype(bfloat)
    grad_queries = (
        jnp.einsum(
            "shqk,skhe->sqhe", grad_scores, key_heads, preferred_element_type=single_layer_input
        )
        * score_scale
    )
    grad_keys = (
        jnp.einsum(
            "shqk,sqhe->skhe", grad_scores, queries, preferred_element_type=single_layer_input
        )
        * score_scale
    )
    grad_values = jnp.einsum(
        "shqk,sqhe->skhe", attention_low, grad_attended, preferred_element_type=single_layer_input
    )
    projection_output_gradient = (
        jnp.stack([grad_queries, grad_keys, grad_values], axis=2)
        .reshape(latents, LEN, 3 * D)
        .astype(bfloat)
    )
    grad_attend = jnp.einsum(
        "ztm,ztg->mg",
        residual_first,
        projection_output_gradient,
        preferred_element_type=single_layer_input,
    )
    grad_hidden_one = jnp.einsum(
        "hfc,zc->hfz",
        projection_output_gradient,
        attention_weight_whole,
        preferred_element_type=single_layer_input,
    )
    grad_shift_one = jnp.sum(grad_hidden_one, axis=1, keepdims=True)
    grad_scale_one = jnp.sum(grad_hidden_one * normed_one, axis=1, keepdims=True)
    tokens_grad = grad_mixed + normalize_back(
        grad_hidden_one * (1.0 + scale_one), normed_one, spread_one
    )
    grad_modulation = jnp.concatenate(
        [
            grad_shift_one,
            grad_scale_one,
            grad_gate_one,
            grad_shift_two,
            grad_scale_two,
            grad_gate_two,
        ],
        axis=2,
    )[:, 0, :].astype(bfloat)
    grad_modulate = jnp.einsum(
        "sd,se->de", cond_low, grad_modulation, preferred_element_type=single_layer_input
    )
    grad_cond_low = jnp.einsum(
        "se,de->sd", grad_modulation, modulate_full, preferred_element_type=single_layer_input
    )
    condition_grad = silu_back(grad_cond_low)[0]
    grad_bias = jnp.concatenate(
        [
            jnp.sum(grad_modulation, axis=0, dtype=single_layer_input),
            jnp.sum(preactivation_gradient, axis=(0, 1), dtype=single_layer_input),
            jnp.sum(branch_gradient, axis=(0, 1), dtype=single_layer_input),
        ]
    )
    totals = lax.psum(
        (
            grad_attend,
            grad_project,
            widening_gradient,
            narrowing_gradient,
            grad_modulate,
            grad_bias,
        ),
        "rep",
    )
    shares = (
        lax.psum_scatter(totals[0], "shard", scatter_dimension=1, tiled=True),
        lax.psum_scatter(totals[1], "shard", scatter_dimension=1, tiled=True),
        lax.psum_scatter(totals[2], "shard", scatter_dimension=1, tiled=True),
        lax.psum_scatter(totals[3], "shard", scatter_dimension=1, tiled=True),
        lax.psum_scatter(totals[4], "shard", scatter_dimension=1, tiled=True),
        lax.psum_scatter(totals[5], "shard", scatter_dimension=0, tiled=True),
    )
    gradients = [shares[0], shares[1], shares[2], shares[3], shares[4]]
    bias_gradient = shares[5]
    masters = [attend_weight, project_weight, expand_weight, contract_weight, modulate_weight]
    moments = [attend_moment, project_moment, expand_moment, contract_moment, modulate_moment]
    momenta = [MOMENTUM * moment_old + gradient for moment_old, gradient in zip(moments, gradients)]
    nesterov = [
        gradient + MOMENTUM * moment_new for gradient, moment_new in zip(gradients, momenta)
    ]
    ortho = owner_orthogonalize(nesterov)
    updated = []
    for master, direction in zip(masters, ortho):
        full_columns = master.shape[1] * lax.axis_size("shard")
        updated.append(
            master * (1.0 - MUON_RATE * WEIGHT_DECAY)
            - MUON_RATE * 0.2 * math.sqrt(full_columns) * direction
        )
    bias_momentum = BETA_ONE * bias_first + (1.0 - BETA_ONE) * bias_gradient
    bias_variance = BETA_TWO * bias_second + (1.0 - BETA_TWO) * bias_gradient * bias_gradient
    corrected_first = bias_momentum / (1.0 - BETA_ONE**STEP)
    corrected_second = bias_variance / (1.0 - BETA_TWO**STEP)
    bias_updated = biases * (1.0 - ADAM_RATE * WEIGHT_DECAY) - ADAM_RATE * corrected_first / (
        jnp.sqrt(corrected_second) + ADAM_EPSILON
    )
    return (
        block_output,
        tokens_grad,
        condition_grad,
        gradients[0],
        gradients[1],
        gradients[2],
        gradients[3],
        gradients[4],
        momenta[0],
        momenta[1],
        momenta[2],
        momenta[3],
        momenta[4],
        updated[0],
        updated[1],
        updated[2],
        updated[3],
        updated[4],
        bias_gradient,
        bias_momentum,
        bias_variance,
        bias_updated,
    )


def solution(mesh):
    placed = (
        P(("shard", "rep"), None, None),
        P(("shard", "rep"), None),
        P(("shard", "rep"), None, None),
        P(None, "shard"),
        P(None, "shard"),
        P(None, "shard"),
        P(None, "shard"),
        P(None, "shard"),
        P("shard"),
        P(None, "shard"),
        P(None, "shard"),
        P(None, "shard"),
        P(None, "shard"),
        P(None, "shard"),
        P("shard"),
        P("shard"),
    )
    return jax.shard_map(
        per_device,
        mesh=mesh,
        in_specs=placed,
        out_specs=(
            P(("shard", "rep"), None, None),
            P(("shard", "rep"), None, None),
            P(("shard", "rep"), None),
            P(None, "shard"),
            P(None, "shard"),
            P(None, "shard"),
            P(None, "shard"),
            P(None, "shard"),
            P(None, "shard"),
            P(None, "shard"),
            P(None, "shard"),
            P(None, "shard"),
            P(None, "shard"),
            P(None, "shard"),
            P(None, "shard"),
            P(None, "shard"),
            P(None, "shard"),
            P(None, "shard"),
            P("shard"),
            P("shard"),
            P("shard"),
            P("shard"),
        ),
        check_vma=False,
    )
```

profile of v0, /device:TPU:0, one launch (start us, length us, event | category | flops | bytes accessed | tf_op | source)
XLA Modules:
  0.0 954.3 jit_solution(6106352371576966381)
XLA Ops:
  13.9 20.9 %all-reduce.13 = bf16[4224]{0:T(1024)(128)(2,1)S(1)} all-reduce(bf16[4224]{0:T(1024)(128)(2,1)S(1)} %dynamic-update-slice), channel_id=1, replica_groups=mesh['shard'=4,'rep'=8] {'shard'}, use_global_device_ids=true, to_apply=%add.13 | all-reduce | flops 4224 | bytes 16896
  36.1 31.7 %all_gather.20 = bf16[384,1152]{0,1:T(8,128)(2,1)S(1)} all-gather(bf16[384,288]{0,1:T(8,128)(2,1)S(1)} %convert_element_type.105), channel_id=1, replica_groups=mesh['shard'=4,'rep'=8] {'shard'}, dimensions={1}, use_global_device_ids=true | all-gather | bytes 1105920 | tf_op jit(solution)/shard_map/all_gather | solution.py:157
  67.9 14.5 %all_gather.21 = bf16[384,384]{0,1:T(8,128)(2,1)S(1)} all-gather(bf16[384,96]{0,1:T(8,128)(2,1)S(1)} %convert_element_type.111), channel_id=1, replica_groups=mesh['shard'=4,'rep'=8] {'shard'}, dimensions={1}, use_global_device_ids=true | all-gather | bytes 368640 | tf_op jit(solution)/shard_map/all_gather | solution.py:158
  99.4 8.2 multiply_convert_fusion.1
  107.6 24.3 %all-gather.8.cloned.1.call-done = bf16[384,1536]{1,0:T(8,128)(2,1)} async-done(((bf16[384,384]{1,0:T(8,128)(2,1)}), bf16[384,1536]{1,0:T(8,128)(2,1)}) %all-gather.8.cloned.1.call-update) | async-done | bytes 1179664 | tf_op jit(solution)/shard_map/all_gather | solution.py:160
  131.9 8.3 convert_reduce_fusion
  194.6 28.3 %reduce-scatter.6.cloned.1.call-done = f32[384,288]{0,1:T(8,128)} async-done(((f32[384,1152]{0,1:T(8,128)}), f32[384,288]{0,1:T(8,128)}) %reduce-scatter.6.cloned.1.call-update) | async-done | bytes 442384 | tf_op jit(solution)/shard_map/reduce_scatter | solution.py:368
  222.9 49.4 %reduce-scatter.10.cloned.1.call-done = f32[384,384]{0,1:T(8,128)} async-done(((f32[384,1536]{0,1:T(8,128)}), f32[384,384]{0,1:T(8,128)}) %reduce-scatter.10.cloned.1.call-update) | async-done | bytes 589840 | tf_op jit(solution)/shard_map/reduce_scatter | solution.py:370
  272.3 50.0 %reduce-scatter.12.cloned.1.call-done = f32[384,384]{0,1:T(8,128)} async-done(((f32[384,1536]{0,1:T(8,128)}), f32[384,384]{0,1:T(8,128)}) %reduce-scatter.12.cloned.1.call-update) | async-done | bytes 589840 | tf_op jit(solution)/shard_map/reduce_scatter | solution.py:371
  322.3 68.3 %reduce-scatter.14.cloned.1.call-done = f32[384,576]{0,1:T(8,128)} async-done(((f32[384,2304]{0,1:T(8,128)}), f32[384,576]{0,1:T(8,128)}) %reduce-scatter.14.cloned.1.call-update) | async-done | bytes 884752 | tf_op jit(solution)/shard_map/reduce_scatter | solution.py:372
  391.1 70.7 %all-reduce.18.cloned.1.call-done = (f32[384,288]{0,1:T(8,128)}, f32[384,96]{0,1:T(8,128)}, f32[384,384]{0,1:T(8,128)}, f32[384,384]{0,1:T(8,128)}, f32[384,576]{0,1:T(8,128)}) async-done(((f32[384,288]{0,1:T(8,128)}, f32[384,96]{0,1:T(8,128)}, f32[384,384]{0,1:T(8,128)}, f32[384,384]{0,1:T(8,128)}, f32[384,576]{0,1:T(8,128)}), (f32[384,288]{0,1:T(8,128)}, f32[384,96]{0,1:T(8,128)}, f32[384,384]{0,1:T(8,128)}, ...) | async-done | bytes 2654224 | tf_op jit(solution)/shard_map/psum | solution.py:356
  476.2 116.9 %all-to-all-done = f32[4,384,864]{1,2,0:T(8,128)} async-done(((f32[4,384,864]{1,2,0:T(8,128)}), f32[4,384,864]{1,2,0:T(8,128)}, u32[]{:S(2)}, u32[]{:S(2)}) %all-to-all-start) | async-done | bytes 5308448 | tf_op jit(solution)/shard_map/all_to_all | solution.py:86
  593.1 174.8 %conditional.1 = (f32[4,384,864]{2,1,0:T(8,128)}) conditional(s32[]{:T(128)} %clamp.3, f32[4,384,864]{1,2,0:T(8,128)} %all-to-all-done, f32[4,384,864]{1,2,0:T(8,128)} %all-to-all-done, f32[4,384,864]{1,2,0:T(8,128)} %all-to-all-done, f32[4,384,864]{1,2,0:T(8,128)} %all-to-all-done), branch_computations={%region_27.0_spmd, %region_30.32_spmd, %region_32.34_spmd, %region... | conditional | flops 67977363456 | bytes 216465728 | solution.py:118
  673.6 6.5 convolution_add_fusion.4
  680.2 5.9 fusion.129
  687.4 6.3 convolution_add_fusion.3
  693.7 5.9 fusion.130
  700.9 6.3 convolution_add_fusion.2
  707.2 5.9 fusion.131
  714.4 6.5 convolution_add_fusion.1
  728.2 6.3 convolution_add_fusion
  767.9 6.1 copy.160
  783.7 121.5 %all-reduce.14 = f32[4224]{0:T(1024)} all-reduce(f32[4224]{0:T(1024)} %pad_maximum_fusion.9), channel_id=7, replica_groups=mesh['shard'=4,'rep'=8] {'shard'}, use_global_device_ids=true, to_apply=%region_40.41.clone | all-reduce | flops 4224 | bytes 33792
  906.5 12.7 %psum.53 = f32[1056]{0:T(1024)} all-reduce(f32[1056]{0:T(1024)} %dynamic-slice.2), channel_id=1, replica_groups=mesh['shard'=4,'rep'=8] {'rep'}, use_global_device_ids=true, to_apply=%region_39.40 | all-reduce | flops 1056 | bytes 8448 | tf_op jit(solution)/shard_map/psum | solution.py:356
  (301 shorter events, 227.4 us)
Async XLA Ops:
  7.2 75.2 %all-gather.4.cloned.1.call-start = ((), (), s32[]{:S(2)}) async-start(), calls=%async_computation.7 | async-start | bytes 2211840 | tf_op jit(solution)/shard_map/all_gather | solution.py:161
  9.4 90.0 %all-gather.6.cloned.1.call-start = ((), (), s32[]{:S(2)}) async-start(), calls=%async_computation.8 | async-start | bytes 1474560 | tf_op jit(solution)/shard_map/all_gather | solution.py:159
  11.3 56.6 %copy-start.49 = (f32[384,96]{0,1:T(8,128)S(1)}, f32[384,96]{0,1:T(8,128)}, u32[]{:S(2)}) copy-start(f32[384,96]{0,1:T(8,128)} %param.24) | copy-start | bytes 442372
  11.3 120.6 %all-gather.8.cloned.1.call-start = ((), (), s32[]{:S(2)}) async-start(), calls=%async_computation.9 | async-start | bytes 1474560 | tf_op jit(solution)/shard_map/all_gather | solution.py:160
  12.1 70.3 %copy-start.61 = (bf16[4,384]{1,0:T(4,128)(2,1)S(1)}, bf16[4,384]{1,0:T(4,128)(2,1)}, u32[]{:S(2)}) copy-start(bf16[4,384]{1,0:T(4,128)(2,1)} %param.21) | copy-start | bytes 9220
  12.2 182.5 %reduce-scatter.8.cloned.1.call-start = ((), (), s32[]{:S(2)}) async-start(), calls=%async_computation.11 | async-start | bytes 737280 | tf_op jit(solution)/shard_map/reduce_scatter | solution.py:369
  35.6 149.5 %copy-start.57 = (f32[4,256]{1,0:T(4,128)}, f32[4,256]{1,0:T(4,128)S(1)}, u32[]{:S(2)}) copy-start(f32[4,256]{1,0:T(4,128)S(1)} %broadcast_multiply_fusion.5) | copy-start | bytes 12292
  36.1 149.0 %copy-start.64 = (f32[4,256]{1,0:T(4,128)}, f32[4,256]{1,0:T(4,128)S(1)}, u32[]{:S(2)}) copy-start(f32[4,256]{1,0:T(4,128)S(1)} %add_rsqrt_fusion.1) | copy-start | bytes 12292
  84.5 100.6 %copy-start.63 = (f32[4,384]{1,0:T(4,128)}, f32[4,384]{1,0:T(4,128)S(1)}, u32[]{:S(2)}) copy-start(f32[4,384]{1,0:T(4,128)S(1)} %get-tuple-element.212) | copy-start | bytes 18436
  90.5 62.2 %copy-start.1 = (bf16[4,256,1152]{1,2,0:T(8,128)(2,1)}, bf16[4,256,1152]{1,2,0:T(8,128)(2,1)S(1)}, u32[]{:S(2)}) copy-start(bf16[4,256,1152]{1,2,0:T(8,128)(2,1)S(1)} %copy.137) | copy-start | bytes 7077892
  162.1 60.8 %reduce-scatter.6.cloned.1.call-start = ((), (), s32[]{:S(2)}) async-start(), calls=%async_computation.10 | async-start | bytes 2211840 | tf_op jit(solution)/shard_map/reduce_scatter | solution.py:368
  173.2 99.1 %reduce-scatter.10.cloned.1.call-start = ((), (), s32[]{:S(2)}) async-start(), calls=%async_computation.12 | async-start | bytes 2949120 | tf_op jit(solution)/shard_map/reduce_scatter | solution.py:370
  178.7 143.6 %reduce-scatter.12.cloned.1.call-start = ((), (), s32[]{:S(2)}) async-start(), calls=%async_computation.13 | async-start | bytes 2949120 | tf_op jit(solution)/shard_map/reduce_scatter | solution.py:371
  185.1 205.5 %reduce-scatter.14.cloned.1.call-start = ((), (), s32[]{:S(2)}) async-start(), calls=%async_computation.14 | async-start | bytes 4423680 | tf_op jit(solution)/shard_map/reduce_scatter | solution.py:372
  194.5 196.1 %copy-start.51 = (f32[384,384]{1,0:T(8,128)S(1)}, f32[384,384]{1,0:T(8,128)}, u32[]{:S(2)}) copy-start(f32[384,384]{1,0:T(8,128)} %param.32) | copy-start | bytes 1769476
  194.5 196.3 %copy-start.52 = (f32[384,384]{1,0:T(8,128)S(1)}, f32[384,384]{1,0:T(8,128)}, u32[]{:S(2)}) copy-start(f32[384,384]{1,0:T(8,128)} %param.31) | copy-start | bytes 1769476
  194.5 267.3 %all-reduce.18.cloned.1.call-start = ((), (), s32[]{:S(2)}) async-start(), calls=%async_computation.15 | async-start | bytes 5308416 | tf_op jit(solution)/shard_map/psum | solution.py:356
  471.1 122.0 %all-to-all-start = ((f32[4,384,864]{1,2,0:T(8,128)}), f32[4,384,864]{1,2,0:T(8,128)}, u32[]{:S(2)}, u32[]{:S(2)}) async-start(f32[4,384,864]{1,2,0:T(8,128)} %pad_maximum_fusion.7), calls=%async_computation | async-start | bytes 10616832 | tf_op jit(solution)/shard_map/all_to_all | solution.py:86
  774.0 159.3 %all-to-all-start.1 = ((f32[4,384,864]{1,2,0:T(8,128)}), f32[4,384,864]{1,2,0:T(8,128)}, u32[]{:S(2)}, u32[]{:S(2)}) async-start(f32[4,384,864]{1,2,0:T(8,128)} %copy.160), calls=%async_computation.1 | async-start | bytes 10616832 | tf_op jit(solution)/shard_map/all_to_all | solution.py:121
  779.2 141.5 %copy-start.60 = (f32[1056]{0:T(1024)S(1)}, f32[1056]{0:T(1024)}, u32[]{:S(2)}) copy-start(f32[1056]{0:T(1024)} %param.28) | copy-start | bytes 12676
  779.2 142.8 %copy-start.62 = (bf16[4,384]{1,0:T(4,128)(2,1)S(1)}, bf16[4,384]{1,0:T(4,128)(2,1)}, u32[]{:S(2)}) copy-start(bf16[4,384]{1,0:T(4,128)(2,1)} %param.21) | copy-start | bytes 9220
  779.3 145.3 %copy-start.3 = (f32[4,256,384]{2,1,0:T(8,128)S(1)}, f32[4,256,384]{2,1,0:T(8,128)}, u32[]{:S(2)}) copy-start(f32[4,256,384]{2,1,0:T(8,128)} %copy-done.2) | copy-start | bytes 4718596
  779.3 145.3 %copy-start.6 = (bf16[4,256,384]{2,1,0:T(8,128)(2,1)S(1)}, bf16[4,256,384]{2,1,0:T(8,128)(2,1)}, u32[]{:S(2)}) copy-start(bf16[4,256,384]{2,1,0:T(8,128)(2,1)} %param.20) | copy-start | bytes 2359300
  779.3 145.3 %copy-start.58 = (f32[4,256]{1,0:T(4,128)S(1)}, f32[4,256]{1,0:T(4,128)}, u32[]{:S(2)}) copy-start(f32[4,256]{1,0:T(4,128)} %copy-done.57) | copy-start | bytes 12292
  (58 other events, 275.4 us)
Sparse Core Ops, SparseCore 0:
  10.2 57.9 all-gather.3
  70.4 28.9 all-gather.5
  101.6 30.2 all-gather.7
  162.2 21.7 reduce-scatter.7
  186.1 36.6 reduce-scatter.5
  225.1 47.1 reduce-scatter.9
  274.7 47.5 reduce-scatter.11
  324.7 65.8 reduce-scatter.13
  395.0 66.7 all-reduce.17
where the time goes:
time: 959 us; the launch traced here: 954 us
  waiting for transfers between devices  409 us (43%)
  blocking collectives  201 us (21%)
  matrix products  179 us (19%)
  local copies, waits for them, and re-layouts  73.4 us (8%)
  other arithmetic  35.3 us (4%)
  loops' own time  29.3 us (3%)
  between operations  16.2 us (2%)
  starting transfers between devices  11.1 us (1%)
    unnamed x2, blocking collectives  142 us
    all_to_all x1, waiting for transfers between devices, owner_orthogonalize(): lax.all_to_all(outgoing, 'shard', split_axis=0, concat_axis=0, tiled=True)  117 us
    psum x1, waiting for transfers between devices, per_device(): lax.psum((grad_attend, grad_project, widening_gradient, narrowing_gradien...  70.7 us
    reduce_scatter x1, waiting for transfers between devices, per_device(): lax.psum_scatter(totals[4], 'shard', scatter_dimension=1, tiled=True)  68.3 us
    reduce_scatter x1, waiting for transfers between devices, per_device(): lax.psum_scatter(totals[3], 'shard', scatter_dimension=1, tiled=True)  50 us
    reduce_scatter x1, waiting for transfers between devices, per_device(): lax.psum_scatter(totals[2], 'shard', scatter_dimension=1, tiled=True)  49.4 us
    dot_general x10, matrix products, poly_step(): jnp.dot(mixing, column_block, precision=EXACT_PRECISION)  48.2 us
    dot_general x10, matrix products, newton_schulz(): gram = jnp.einsum('rc,dc->rd', current, current, precision=EXACT_PRECISION)  46.1 us
  transfers between devices with their start and end apart: 11, of which 8 were waited for; matrix products, arithmetic and copies ran while one was open for 8% of the time, Pallas kernels for 0%

commit v1 on v0

--- a/solution.py
+++ b/solution.py
@@ -42,19 +42,6 @@
     )
 
 
-def poly_step(column_block, gram):
-    mixing = POLY_CUBIC * gram + POLY_QUINTIC * jnp.dot(gram, gram, precision=EXACT_PRECISION)
-    return POLY_LINEAR * column_block + jnp.dot(mixing, column_block, precision=EXACT_PRECISION)
-
-
-def newton_schulz(matrix):
-    current = matrix / (jnp.sqrt(jnp.sum(matrix * matrix)) + 1e-07)
-    for iteration in range(NS_ITERS):
-        gram = jnp.einsum("rc,dc->rd", current, current, precision=EXACT_PRECISION)
-        current = poly_step(current, gram)
-    return current
-
-
 def pad_columns(blocks, width, rows):
     filled = sum((block.shape[1] for block in blocks))
     if filled < width:
@@ -62,67 +49,171 @@
     return jnp.concatenate(blocks, axis=1)
 
 
-def owner_orthogonalize(column_shares):
-    devices = lax.axis_size("shard")
-    widths = [share.shape[1] for share in column_shares]
-    owned = [
-        [number for number in range(len(column_shares)) if number % devices == owner]
-        for owner in range(devices)
-    ]
-    offsets = {}
-    for owner in range(devices):
-        running = 0
-        for number in owned[owner]:
-            offsets[number] = running
-            running = running + widths[number]
-    slot_width = max((sum((widths[number] for number in members)) for members in owned))
-    outgoing = jnp.stack(
+def shift(value, distance):
+    size = lax.axis_size("shard")
+    return lax.ppermute(value, "shard", [(i, (i + distance) % size) for i in range(size)])
+
+
+def flip(value, bit):
+    size = lax.axis_size("rep")
+    return lax.ppermute(value, "rep", [(i, i ^ (1 << bit)) for i in range(size)])
+
+
+def bit_orders():
+    count = lax.axis_size("rep").bit_length() - 1
+    outer = list(range(1, count))
+    return (outer + [0], outer[::-1] + [0])
+
+
+def relative_order(bits):
+    order = [0]
+    for bit in bits:
+        order = order + [j ^ (1 << bit) for j in order]
+    return order
+
+
+def gather_rep(value, bits):
+    value = value[None]
+    for bit in bits:
+        value = jnp.concatenate([value, flip(value, bit)], axis=0)
+    return value
+
+
+def reduce_rep(value, bits):
+    for bit in reversed(bits):
+        half = value.shape[0] // 2
+        received = flip(value[half:].astype(jnp.bfloat16), bit)
+        value = value[:half] + received.astype(jnp.float32)
+    return value[0]
+
+
+def gather_weights(blocks):
+    shards, reps = lax.axis_size("shard"), lax.axis_size("rep")
+    shard, rep = lax.axis_index("shard"), lax.axis_index("rep")
+    rows = D // reps
+    packed = jnp.concatenate(
+        [lax.dynamic_slice_in_dim(block, rep * rows, rows, 0).astype(jnp.bfloat16) for block in blocks],
+        axis=1,
+    )
+    pieces = jnp.stack([packed] + [shift(packed, d) for d in range(1, shards)])
+    middle = (shards + 1) // 2
+    full = []
+    for part, bits in zip((pieces[:middle], pieces[middle:]), bit_orders()):
+        gathered = gather_rep(part, bits)
+        order = jnp.array(relative_order(bits))
+        inverse = jnp.argsort(order)
+        full.append(jnp.take(gathered, jnp.take(inverse, rep ^ jnp.arange(reps)), axis=0))
+    full = jnp.concatenate(full, axis=1)
+    full = jnp.take(full, (shard - jnp.arange(shards)) % shards, axis=1)
+    full = full.transpose(0, 2, 1, 3).reshape(D, shards, packed.shape[1])
+    results, start = [], 0
+    for block in blocks:
+        width = block.shape[1]
+        results.append(full[:, :, start : start + width].reshape(D, shards * width))
+        start = start + width
+    return results
+
+
+def reduce_gradients(matrices):
+    shards, reps = lax.axis_size("shard"), lax.axis_size("rep")
+    shard, rep = lax.axis_index("shard"), lax.axis_index("rep")
+    rows = D // reps
+    packed = jnp.concatenate(
+        [m.reshape(reps, rows, shards, m.shape[1] // shards) for m in matrices], axis=3
+    ).transpose(0, 2, 1, 3)
+    packed = jnp.take(packed, (shard + jnp.arange(shards)) % shards, axis=1)
+    middle = (shards + 1) // 2
+    mine = []
+    for part, bits in zip((packed[:, :middle], packed[:, middle:]), bit_orders()):
+        order = jnp.array(relative_order(bits))
+        mine.append(reduce_rep(jnp.take(part, rep ^ order, axis=0), bits))
+    mine = jnp.concatenate(mine, axis=0)
+    total = mine[0]
+    for d in range(1, shards):
+        total = total + shift(mine[d].astype(jnp.bfloat16), d).astype(jnp.float32)
+    bits = bit_orders()[0]
+    gathered = gather_rep(total.astype(jnp.bfloat16), bits)
+    inverse = jnp.argsort(jnp.array(relative_order(bits)))
+    whole = jnp.take(gathered, jnp.take(inverse, rep ^ jnp.arange(reps)), axis=0)
+    whole = whole.reshape(D, -1).astype(jnp.float32)
+    results, start = [], 0
+    for m in matrices:
+        width = m.shape[1] // shards
+        results.append(whole[:, start : start + width])
+        start = start + width
+    return results
+
+
+def exact(left, right):
+    return jnp.dot(left, right, precision=EXACT_PRECISION)
+
+
+SLOTS = ((4, 0, 2), (4, 1, 2), (0, 0, 1), (2, 0, 2), (2, 1, 2), (3, 0, 2), (3, 1, 2), (1, 0, 1))
+
+
+def polynomial(gram):
+    scale = 1.0 / (jnp.sqrt(jnp.trace(gram)) + 1e-07)
+    gram = gram * (scale * scale)
+    product = None
+    for step in range(NS_ITERS):
+        mixing = POLY_CUBIC * gram + POLY_QUINTIC * exact(gram, gram)
+        if step + 1 < NS_ITERS:
+            half = POLY_LINEAR * gram + exact(mixing, gram)
+            gram = POLY_LINEAR * half + exact(mixing, half)
+        if product is None:
+            product = POLY_LINEAR * jnp.eye(D, dtype=jnp.float32) + mixing
+        else:
+            product = POLY_LINEAR * product + exact(mixing, product)
+    return product * scale
+
+
+def orthogonalize(shares):
+    shards, reps = lax.axis_size("shard"), lax.axis_size("rep")
+    shard, rep = lax.axis_index("shard"), lax.axis_index("rep")
+    slot = rep % len(SLOTS)
+    widest = max(share.shape[1] for share in shares)
+    slot_widest = max(shares[m].shape[1] // parts for m, _, parts in SLOTS)
+    padded = jnp.stack([pad_columns([share], widest, D) for share in shares])
+    matrix = lax.dynamic_index_in_dim(
+        padded, jnp.array([m for m, _, _ in SLOTS])[slot], 0, keepdims=False
+    )
+    slots = jnp.stack(
         [
-            pad_columns([column_shares[number] for number in owned[owner]], slot_width, D)
-            for owner in range(devices)
-        ],
-        axis=0,
-    )
-    incoming = lax.all_to_all(outgoing, "shard", split_axis=0, concat_axis=0, tiled=True)
-
-    def owner_work(owner):
-
-        def run(received):
-            results = []
-            for number in owned[owner]:
-                start = offsets[number]
-                whole = jnp.concatenate(
-                    [
-                        received[source][:, start : start + widths[number]]
-                        for source in range(devices)
-                    ],
-                    axis=1,
-                )
-                results.append(newton_schulz(whole))
-            slots = []
-            for source in range(devices):
-                slots.append(
-                    pad_columns(
-                        [
-                            result[:, source * widths[number] : (source + 1) * widths[number]]
-                            for result, number in zip(results, owned[owner])
-                        ],
-                        slot_width,
-                        D,
-                    )
-                )
-            return jnp.stack(slots, axis=0)
-
-        return run
-
-    replies = lax.switch(
-        lax.axis_index("shard"), [owner_work(owner) for owner in range(devices)], incoming
-    )
-    returned = lax.all_to_all(replies, "shard", split_axis=0, concat_axis=0, tiled=True)
-    return [
-        returned[number % devices][:, offsets[number] : offsets[number] + widths[number]]
-        for number in range(len(column_shares))
-    ]
+            pad_columns(
+                [shares[m][:, p * (shares[m].shape[1] // parts) : (p + 1) * (shares[m].shape[1] // parts)]],
+                slot_widest,
+                D,
+            )
+            for m, p, parts in SLOTS
+        ]
+    )
+    columns = lax.dynamic_index_in_dim(slots, slot, 0, keepdims=False)
+    partial_gram = exact(matrix, matrix.T).reshape(shards, D // shards, D)
+    partial_gram = jnp.take(partial_gram, (shard + jnp.arange(shards)) % shards, axis=0)
+    piece = partial_gram[0]
+    for d in range(1, shards):
+        piece = piece + shift(partial_gram[d], d)
+    gram = jnp.stack([piece] + [shift(piece, d) for d in range(1, shards)])
+    gram = jnp.take(gram, (shard - jnp.arange(shards)) % shards, axis=0).reshape(D, D)
+    answer = exact(polynomial(gram), columns).astype(jnp.bfloat16)
+    bits = [b for b in bit_orders()[0] if (1 << b) < len(SLOTS)]
+    gathered = gather_rep(answer, bits)
+    order = relative_order(bits)
+    inverse = jnp.argsort(jnp.array(order))
+    whole = jnp.take(gathered, jnp.take(inverse, slot ^ jnp.arange(len(SLOTS))), axis=0)
+    results = []
+    for number, share in enumerate(shares):
+        results.append(
+            jnp.concatenate(
+                [
+                    whole[k][:, : share.shape[1] // parts]
+                    for k, (m, p, parts) in enumerate(SLOTS)
+                    if m == number
+                ],
+                axis=1,
+            ).astype(jnp.float32)
+        )
+    return results
 
 
 def per_device(
@@ -146,30 +237,28 @@
     bfloat = jnp.bfloat16
     single_layer_input = jnp.float32
     latents = tokens.shape[0]
-    (
-        attention_weight_whole,
-        projection_weight_whole,
-        widening_weight_whole,
-        narrowing_weight_whole,
-        modulate_full,
-        bias_full,
-    ) = (
-        lax.all_gather(attend_weight.astype(bfloat), "shard", axis=1, tiled=True),
-        lax.all_gather(project_weight.astype(bfloat), "shard", axis=1, tiled=True),
-        lax.all_gather(expand_weight.astype(bfloat), "shard", axis=1, tiled=True),
-        lax.all_gather(contract_weight.astype(bfloat), "shard", axis=1, tiled=True),
-        lax.all_gather(modulate_weight.astype(bfloat), "shard", axis=1, tiled=True),
-        lax.all_gather(biases.astype(bfloat), "shard", axis=0, tiled=True),
-    )
+    shards, reps = lax.axis_size("shard"), lax.axis_size("rep")
+    shard, rep = lax.axis_index("shard"), lax.axis_index("rep")
+    attention_weight_whole, projection_weight_whole = gather_weights([attend_weight, project_weight])
+    widening_weight_whole, narrowing_weight_whole = gather_weights([expand_weight, contract_weight])
+    modulate_low = modulate_weight.astype(bfloat)
+    bias_low = biases.astype(bfloat)
+    bias_pieces = jnp.stack([bias_low] + [shift(bias_low, d) for d in range(1, shards)])
+    source_order = (shard - jnp.arange(shards)) % shards
+    bias_full = jnp.take(bias_pieces, source_order, axis=0).reshape(-1)
     ada_bias = bias_full[: 6 * D].astype(single_layer_input)
     widening_bias = bias_full[6 * D : 6 * D + FF].astype(single_layer_input)
     narrowing_bias = bias_full[6 * D + FF :].astype(single_layer_input)
     inputs = tokens.astype(single_layer_input)
     silu_value, silu_back = jax.vjp(jax.nn.silu, condition.astype(single_layer_input))
     cond_low = silu_value.astype(bfloat)
-    modulation = (
-        jnp.dot(cond_low, modulate_full, preferred_element_type=single_layer_input) + ada_bias
-    )
+    cond_pieces = jnp.stack([cond_low] + [shift(cond_low, d) for d in range(1, shards)])
+    share = jnp.dot(
+        cond_pieces.reshape(shards * latents, D), modulate_low, preferred_element_type=single_layer_input
+    ).reshape(shards, latents, -1)
+    answers = jnp.stack([share[0]] + [shift(share[d], shards - d) for d in range(1, shards)])
+    answers = jnp.take(answers, (jnp.arange(shards) - shard) % shards, axis=0)
+    modulation = answers.transpose(1, 0, 2).reshape(latents, 6 * D) + ada_bias
     shift_one, scale_one, gate_one, shift_two, scale_two, gate_two = jnp.split(
         modulation[:, None, :], 6, axis=2
     )
@@ -339,12 +428,24 @@
         ],
         axis=2,
     )[:, 0, :].astype(bfloat)
+    outgoing = grad_modulation.reshape(latents, shards, -1).transpose(1, 0, 2)
+    outgoing = jnp.take(outgoing, (shard + jnp.arange(shards)) % shards, axis=0)
+    received = jnp.stack([outgoing[0]] + [shift(outgoing[d], d) for d in range(1, shards)])
+    bits = bit_orders()[0]
+    grad_columns = gather_rep(received.reshape(shards * latents, -1), bits)
+    cond_all = gather_rep(cond_pieces.reshape(shards * latents, D), bits)
     grad_modulate = jnp.einsum(
-        "sd,se->de", cond_low, grad_modulation, preferred_element_type=single_layer_input
-    )
-    grad_cond_low = jnp.einsum(
-        "se,de->sd", grad_modulation, modulate_full, preferred_element_type=single_layer_input
-    )
+        "rsd,rse->de", cond_all, grad_columns, preferred_element_type=single_layer_input
+    )
+    grad_cond_share = jnp.einsum(
+        "se,de->sd",
+        received.reshape(shards * latents, -1),
+        modulate_low,
+        preferred_element_type=single_layer_input,
+    ).reshape(shards, latents, D)
+    grad_cond_low = grad_cond_share[0]
+    for d in range(1, shards):
+        grad_cond_low = grad_cond_low + shift(grad_cond_share[d], shards - d)
     condition_grad = silu_back(grad_cond_low)[0]
     grad_bias = jnp.concatenate(
         [
@@ -353,34 +454,24 @@
             jnp.sum(branch_gradient, axis=(0, 1), dtype=single_layer_input),
         ]
     )
-    totals = lax.psum(
-        (
-            grad_attend,
-            grad_project,
-            widening_gradient,
-            narrowing_gradient,
-            grad_modulate,
-            grad_bias,
-        ),
-        "rep",
-    )
-    shares = (
-        lax.psum_scatter(totals[0], "shard", scatter_dimension=1, tiled=True),
-        lax.psum_scatter(totals[1], "shard", scatter_dimension=1, tiled=True),
-        lax.psum_scatter(totals[2], "shard", scatter_dimension=1, tiled=True),
-        lax.psum_scatter(totals[3], "shard", scatter_dimension=1, tiled=True),
-        lax.psum_scatter(totals[4], "shard", scatter_dimension=1, tiled=True),
-        lax.psum_scatter(totals[5], "shard", scatter_dimension=0, tiled=True),
-    )
-    gradients = [shares[0], shares[1], shares[2], shares[3], shares[4]]
-    bias_gradient = shares[5]
+    grad_expand, grad_contract = reduce_gradients([widening_gradient, narrowing_gradient])
+    grad_attend, grad_project = reduce_gradients([grad_attend, grad_project])
+    gradients = [grad_attend, grad_project, grad_expand, grad_contract, grad_modulate]
+    bias_parts = jnp.take(
+        grad_bias.reshape(shards, -1), (shard + jnp.arange(shards)) % shards, axis=0
+    )
+    bias_gradient = bias_parts[0]
+    for d in range(1, shards):
+        bias_gradient = bias_gradient + shift(bias_parts[d], d)
+    for bit in bits:
+        bias_gradient = bias_gradient + flip(bias_gradient, bit)
     masters = [attend_weight, project_weight, expand_weight, contract_weight, modulate_weight]
     moments = [attend_moment, project_moment, expand_moment, contract_moment, modulate_moment]
     momenta = [MOMENTUM * moment_old + gradient for moment_old, gradient in zip(moments, gradients)]
     nesterov = [
         gradient + MOMENTUM * moment_new for gradient, moment_new in zip(gradients, momenta)
     ]
-    ortho = owner_orthogonalize(nesterov)
+    ortho = orthogonalize(nesterov)
     updated = []
     for master, direction in zip(masters, ortho):
         full_columns = master.shape[1] * lax.axis_size("shard")

time: 959 us -> 441 us (0.46)
  waiting for transfers between devices: 409 us -> 69.8 us
  blocking collectives: 201 us -> 0 us
  matrix products: 179 us -> 79.9 us
  starting transfers between devices: 11.1 us -> 91 us
  local copies, waits for them, and re-layouts: 73.4 us -> 117 us
  other arithmetic: 35.3 us -> 70.2 us
  loops' own time: 29.3 us -> 0 us
  between operations: 16.2 us -> 5.86 us
    reduce_scatter x5 -> x0, waiting for transfers between devices: 196 us -> none  [the longest x1 68.3 us: per_device(): lax.psum_scatter(totals[4], 'shard', scatter_dimension=1, tiled=True)]
    unnamed x2 -> x0, blocking collectives: 142 us -> none
    all_to_all x2 -> x0, waiting for transfers between devices: 117 us -> none  [the longest x1 117 us: owner_orthogonalize(): lax.all_to_all(outgoing, 'shard', split_axis=0, concat_axis=0, tiled=True)]
    ppermute x0 -> x78, starting transfers between devices: none -> 91 us  [the longest x36 56.3 us: shift(): lax.ppermute(value, 'shard', [(i, (i + distance) % size) for i in range(s...]
    dot_general x33 -> x22, matrix products: 114 us -> 29.8 us  [the longest x19 26.5 us: exact(): return jnp.dot(left, right, precision=EXACT_PRECISION)]
    psum x1 -> x0, waiting for transfers between devices: 70.7 us -> none  [per_device(): lax.psum((grad_attend, grad_project, widening_gradient, narrowing_gradien...]
    ppermute x0 -> x78, waiting for transfers between devices: none -> 69.8 us  [the longest x42 44.6 us: flip(): return lax.ppermute(value, 'rep', [(i, i ^ 1 << bit) for i in range(size)])]
    all_gather x2 -> x0, blocking collectives: 46.2 us -> none  [the longest x1 31.7 us: per_device(): lax.all_gather(attend_weight.astype(bfloat), 'shard', axis=1, tiled=True)]
  transfers between devices with their start and end apart: 11 -> 78, of which waited for: 8 -> 32; matrix products, arithmetic and copies ran while one was open for 8% -> 49% of each run, Pallas kernels for 0% -> 0%
where the time goes in v1:
time: 441 us; the launch traced here: 434 us
  local copies, waits for them, and re-layouts  117 us (27%)
  starting transfers between devices  91 us (21%)
  matrix products  79.9 us (18%)
  other arithmetic  70.2 us (16%)
  waiting for transfers between devices  69.8 us (16%)
  between operations  5.86 us (1%)
    ppermute x36, starting transfers between devices, shift(): lax.ppermute(value, 'shard', [(i, (i + distance) % size) for i in range(s...  56.3 us
    ppermute x42, waiting for transfers between devices, flip(): return lax.ppermute(value, 'rep', [(i, i ^ 1 << bit) for i in range(size)])  44.6 us
    ppermute x42, starting transfers between devices, flip(): return lax.ppermute(value, 'rep', [(i, i ^ 1 << bit) for i in range(size)])  34.7 us
    unnamed x235, local copies, waits for them, and re-layouts  31.7 us
    dot_general x19, matrix products, exact(): return jnp.dot(left, right, precision=EXACT_PRECISION)  26.5 us
    ppermute x36, waiting for transfers between devices, shift(): lax.ppermute(value, 'shard', [(i, (i + distance) % size) for i in range(s...  25.2 us
    concatenate x25, other arithmetic, gather_rep(): value = jnp.concatenate([value, flip(value, bit)], axis=0)  11.4 us
    gather x2, local copies, waits for them, and re-layouts, reduce_gradients(): packed = jnp.take(packed, (shard + jnp.arange(shards)) % shards, axis=1)  9.37 us
  transfers between devices with their start and end apart: 78, of which 32 were waited for; matrix products, arithmetic and copies ran while one was open for 49% of the time, Pallas kernels for 0%

profile of v1, /device:TPU:0, one launch (start us, length us, event | category | flops | bytes accessed | tf_op | source)
XLA Modules:
  0.0 434.1 jit_solution(4765949258769794436)
XLA Ops:
  1.5 4.1 collective-permute-start.1
  32.5 3.3 collective-permute-start.2
  71.6 5.5 %collective-permute-done.25 = bf16[2,2,48,768]{3,2,1,0:T(8,128)(2,1)S(1)} collective-permute-done((bf16[2,2,48,768]{3,2,1,0:T(8,128)(2,1)S(1)}, bf16[2,2,48,768]{3,2,1,0:T(8,128)(2,1)S(1)}, u32[]{:S(2)}, u32[]{:S(2)}) %collective-permute-start.25) | collective-permute-done | bytes 294944 | tf_op jit(solution)/shard_map/ppermute | solution.py:59
  100.8 3.2 gather_fusion.16
  115.1 3.9 gather_fusion.3
  124.1 3.2 reshape.725
  127.3 3.2 copy.248
  130.6 3.3 reshape.724
  134.0 4.3 multiply_convert_fusion.1
  138.3 6.6 %convert_reduce_fusion = (f32[1536]{0:T(1024)}, bf16[4,256,1536]{2,1,0:T(8,128)(2,1)S(1)}) fusion(f32[4,256,1536]{2,1,0:T(8,128)S(1)} %get-tuple-element.228, f32[1536]{0:T(1024)S(1)} %copy-done.89, bf16[384,1536,1]{1,0,2:T(8,128)(2,1)S(1)} %copy-done.45, bf16[4,256,384]{2,1,0:T(8,128)(2,1)S(1)} %copy-done.51, f32[4,384]{1,0:T(4,128)S(1)} %get-tuple-element.211), kind=kOutput, calls=%fused_computation.33 | convolution fusion | flops 1245313536 | bytes 11421696 | tf_op jit(solution)/shard_map/pvk,km->pvm/dot_general | solution.py:330
  152.8 4.1 convert_reduce_fusion.2
  162.0 5.3 %convolution_bitcast_fusion.2 = bf16[4,256,1,6,64]{1,4,3,0,2:T(8,128)(2,1)} fusion(bf16[4,256,6,64]{1,3,2,0:T(8,128)(2,1)} %bitcast.363, f32[4,6,256,256]{2,3,1,0:T(8,128)} %copy-done.1, f32[4,6,256]{2,1,0:T(8,128)S(1)} %log_add_fusion), kind=kOutput, calls=%fused_computation.89 | convolution fusion | flops 206045184 | bytes 7888896 | tf_op jit(solution)/shard_map/shqk,sqhe->skhe/dot_general | solution.py:395
  171.8 3.3 multiply_bitcast_fusion
  178.7 3.5 copy.204
  189.2 5.4 %gather_fusion.7 = f32[4,8,48,768]{3,2,1,0:T(8,128)} fusion(f32[8,4,48,768]{3,2,1,0:T(8,128)} %maximum_bitcast_fusion, s32[1024]{0:T(1024)} %get-tuple-element.241), kind=kCustom, calls=%fused_computation.20 | custom fusion | bytes 9437200 | tf_op jit(solution)/shard_map/jit(_take)/gather | solution.py:124
  219.8 3.9 gather_fusion.5
  262.4 3.6 collective-permute-done.34
  288.4 3.6 collective-permute-done.46
  308.7 3.4 collective-permute-done.54
  341.5 6.4 %collective-permute-done.64 = f32[96,384]{1,0:T(8,128)S(1)} collective-permute-done((f32[96,384]{1,0:T(8,128)S(1)}, f32[96,384]{1,0:T(8,128)S(1)}, u32[]{:S(2)}, u32[]{:S(2)}) %collective-permute-start.64) | collective-permute-done | bytes 147488 | tf_op jit(solution)/shard_map/ppermute | solution.py:54
  351.8 3.3 collective-permute-done.68
  355.1 6.1 %collective-permute-done.67 = f32[96,384]{1,0:T(8,128)S(1)} collective-permute-done((f32[96,384]{1,0:T(8,128)S(1)}, f32[96,384]{1,0:T(8,128)S(1)}, u32[]{:S(2)}, u32[]{:S(2)}) %collective-permute-start.67) | collective-permute-done | bytes 147488 | tf_op jit(solution)/shard_map/ppermute | solution.py:54
  398.4 6.4 %collective-permute-done.70 = bf16[2,384,288]{1,2,0:T(8,128)(2,1)S(1)} collective-permute-done((bf16[2,384,288]{1,2,0:T(8,128)(2,1)S(1)}, bf16[2,384,288]{1,2,0:T(8,128)(2,1)S(1)}, u32[]{:S(2)}, u32[]{:S(2)}) %collective-permute-start.70) | collective-permute-done | bytes 442400 | tf_op jit(solution)/shard_map/ppermute | solution.py:59
  409.5 3.9 collective-permute-start.31
  (648 shorter events, 325.5 us)
Async XLA Ops:
  1.5 37.0 %collective-permute-start.1 = (bf16[4,384]{1,0:T(4,128)(2,1)S(1)}, bf16[4,384]{1,0:T(4,128)(2,1)S(1)}, u32[]{:S(2)}, u32[]{:S(2)}) collective-permute-start(bf16[4,384]{1,0:T(4,128)(2,1)S(1)} %fusion.104), channel_id=1, source_target_pairs={{0,16},{8,24},{16,0},{24,8},{1,17},{9,25},{17,1},{25,9},{2,18},{10... | collective-permute-start | bytes 9224 | tf_op jit(solution)/shard_map/ppermute | solution.py:54
  5.6 32.9 %collective-permute-start = (bf16[4,384]{1,0:T(4,128)(2,1)S(1)}, bf16[4,384]{1,0:T(4,128)(2,1)S(1)}, u32[]{:S(2)}, u32[]{:S(2)}) collective-permute-start(bf16[4,384]{1,0:T(4,128)(2,1)S(1)} %fusion.104), channel_id=1, source_target_pairs={{0,8},{8,16},{16,24},{24,0},{1,9},{9,17},{17,25},{25,1},{2,10},{10... | collective-permute-start | bytes 9224 | tf_op jit(solution)/shard_map/ppermute | solution.py:54
  7.9 24.6 %collective-permute-start.8 = (bf16[1056]{0:T(1024)(128)(2,1)S(1)}, bf16[1056]{0:T(1024)(128)(2,1)S(1)}, u32[]{:S(2)}, u32[]{:S(2)}) collective-permute-start(bf16[1056]{0:T(1024)(128)(2,1)S(1)} %convert_element_type.240), channel_id=1, source_target_pairs={{0,24},{8,0},{16,8},{24,16},{1,25},{9,1},{17,9},{25,17},{2,26},{10... | collective-permute-start | bytes 6344 | tf_op jit(solution)/shard_map/ppermute | solution.py:54
  10.1 25.7 %collective-permute-start.7 = (bf16[1056]{0:T(1024)(128)(2,1)S(1)}, bf16[1056]{0:T(1024)(128)(2,1)S(1)}, u32[]{:S(2)}, u32[]{:S(2)}) collective-permute-start(bf16[1056]{0:T(1024)(128)(2,1)S(1)} %convert_element_type.240), channel_id=1, source_target_pairs={{0,16},{8,24},{16,0},{24,8},{1,17},{9,25},{17,1},{25,9},{2,18},{10... | collective-permute-start | bytes 6344 | tf_op jit(solution)/shard_map/ppermute | solution.py:54
  10.1 26.3 %collective-permute-start.6 = (bf16[1056]{0:T(1024)(128)(2,1)S(1)}, bf16[1056]{0:T(1024)(128)(2,1)S(1)}, u32[]{:S(2)}, u32[]{:S(2)}) collective-permute-start(bf16[1056]{0:T(1024)(128)(2,1)S(1)} %convert_element_type.240), channel_id=1, source_target_pairs={{0,8},{8,16},{16,24},{24,0},{1,9},{9,17},{17,25},{25,1},{2,10},{10... | collective-permute-start | bytes 6344 | tf_op jit(solution)/shard_map/ppermute | solution.py:54
  35.8 19.1 %collective-permute-start.14 = (bf16[48,384]{1,0:T(8,128)(2,1)S(1)}, bf16[48,384]{1,0:T(8,128)(2,1)S(1)}, u32[]{:S(2)}, u32[]{:S(2)}) collective-permute-start(bf16[48,384]{1,0:T(8,128)(2,1)S(1)} %pad_maximum_fusion.29), channel_id=1, source_target_pairs={{0,24},{8,0},{16,8},{24,16},{1,25},{9,1},{17,9},{25,17},{2,26},{10... | collective-permute-start | bytes 110600 | tf_op jit(solution)/shard_map/ppermute | solution.py:54
  36.5 20.1 %collective-permute-start.13 = (bf16[48,384]{1,0:T(8,128)(2,1)S(1)}, bf16[48,384]{1,0:T(8,128)(2,1)S(1)}, u32[]{:S(2)}, u32[]{:S(2)}) collective-permute-start(bf16[48,384]{1,0:T(8,128)(2,1)S(1)} %pad_maximum_fusion.29), channel_id=1, source_target_pairs={{0,16},{8,24},{16,0},{24,8},{1,17},{9,25},{17,1},{25,9},{2,18},{10... | collective-permute-start | bytes 110600 | tf_op jit(solution)/shard_map/ppermute | solution.py:54
  45.5 15.5 %collective-permute-start.22 = (bf16[48,768]{1,0:T(8,128)(2,1)S(1)}, bf16[48,768]{1,0:T(8,128)(2,1)S(1)}, u32[]{:S(2)}, u32[]{:S(2)}) collective-permute-start(bf16[48,768]{1,0:T(8,128)(2,1)S(1)} %get-tuple-element.206), channel_id=1, source_target_pairs={{0,16},{8,24},{16,0},{24,8},{1,17},{9,25},{17,1},{25,9},{2,18},{10... | collective-permute-start | bytes 221192 | tf_op jit(solution)/shard_map/ppermute | solution.py:54
  61.0 194.6 %collective-permute-start.59 = (bf16[4,16,384]{2,1,0:T(8,128)(2,1)}, bf16[4,16,384]{2,1,0:T(8,128)(2,1)}, u32[]{:S(2)}, u32[]{:S(2)}) collective-permute-start(bf16[4,16,384]{2,1,0:T(8,128)(2,1)} %pad_maximum_fusion.26), channel_id=1, source_target_pairs={{0,1},{1,0},{2,3},{3,2},{4,5},{5,4},{6,7},{7,6},{8,9},{9,8},{10,11... | collective-permute-start | bytes 147464 | tf_op jit(solution)/shard_map/ppermute | solution.py:59
  78.1 20.5 %collective-permute-start.26 = (bf16[4,2,48,768]{3,2,1,0:T(8,128)(2,1)}, bf16[4,2,48,768]{3,2,1,0:T(8,128)(2,1)}, u32[]{:S(2)}, u32[]{:S(2)}) collective-permute-start(bf16[4,2,48,768]{3,2,1,0:T(8,128)(2,1)} %pad_maximum_fusion.9), channel_id=1, source_target_pairs={{0,1},{1,0},{2,3},{3,2},{4,5},{5,4},{6,7},{7,6},{8,9},{9,8},{10,11... | collective-permute-start | bytes 1769480 | tf_op jit(solution)/shard_map/ppermute | solution.py:59
  79.0 27.5 %collective-permute-start.21 = (bf16[4,2,48,768]{3,2,1,0:T(8,128)(2,1)}, bf16[4,2,48,768]{3,2,1,0:T(8,128)(2,1)}, u32[]{:S(2)}, u32[]{:S(2)}) collective-permute-start(bf16[4,2,48,768]{3,2,1,0:T(8,128)(2,1)} %pad_maximum_fusion.8), channel_id=1, source_target_pairs={{0,1},{1,0},{2,3},{3,2},{4,5},{5,4},{6,7},{7,6},{8,9},{9,8},{10,11... | collective-permute-start | bytes 1769480 | tf_op jit(solution)/shard_map/ppermute | solution.py:59
  211.1 29.3 %collective-permute-start.29 = (bf16[4,576]{1,0:T(4,128)(2,1)}, bf16[4,576]{1,0:T(4,128)(2,1)}, u32[]{:S(2)}, u32[]{:S(2)}) collective-permute-start(bf16[4,576]{1,0:T(4,128)(2,1)} %get-tuple-element.221), channel_id=1, source_target_pairs={{0,24},{8,0},{16,8},{24,16},{1,25},{9,1},{17,9},{25,17},{2,26},{10... | collective-permute-start | bytes 13832 | tf_op jit(solution)/shard_map/ppermute | solution.py:54
  211.7 28.7 %collective-permute-start.28 = (bf16[4,576]{1,0:T(4,128)(2,1)}, bf16[4,576]{1,0:T(4,128)(2,1)}, u32[]{:S(2)}, u32[]{:S(2)}) collective-permute-start(bf16[4,576]{1,0:T(4,128)(2,1)} %get-tuple-element.222), channel_id=1, source_target_pairs={{0,16},{8,24},{16,0},{24,8},{1,17},{9,25},{17,1},{25,9},{2,18},{10... | collective-permute-start | bytes 13832 | tf_op jit(solution)/shard_map/ppermute | solution.py:54
  212.6 27.8 %collective-permute-start.27 = (bf16[4,576]{1,0:T(4,128)(2,1)}, bf16[4,576]{1,0:T(4,128)(2,1)}, u32[]{:S(2)}, u32[]{:S(2)}) collective-permute-start(bf16[4,576]{1,0:T(4,128)(2,1)} %get-tuple-element.223), channel_id=1, source_target_pairs={{0,8},{8,16},{16,24},{24,0},{1,9},{9,17},{17,25},{25,1},{2,10},{10... | collective-permute-start | bytes 13832 | tf_op jit(solution)/shard_map/ppermute | solution.py:54
  237.9 46.1 %collective-permute-start.45 = (bf16[4,2,48,768]{3,2,1,0:T(8,128)(2,1)}, bf16[4,2,48,768]{3,2,1,0:T(8,128)(2,1)}, u32[]{:S(2)}, u32[]{:S(2)}) collective-permute-start(bf16[4,2,48,768]{3,2,1,0:T(8,128)(2,1)} %slice.667), channel_id=1, source_target_pairs={{0,1},{1,0},{2,3},{3,2},{4,5},{5,4},{6,7},{7,6},{8,9},{9,8},{10,11... | collective-permute-start | bytes 1769480 | tf_op jit(solution)/shard_map/ppermute | solution.py:59
  247.2 38.9 %collective-permute-start.49 = (bf16[4,2,48,768]{3,2,1,0:T(8,128)(2,1)}, bf16[4,2,48,768]{3,2,1,0:T(8,128)(2,1)}, u32[]{:S(2)}, u32[]{:S(2)}) collective-permute-start(bf16[4,2,48,768]{3,2,1,0:T(8,128)(2,1)} %slice.666), channel_id=1, source_target_pairs={{0,1},{1,0},{2,3},{3,2},{4,5},{5,4},{6,7},{7,6},{8,9},{9,8},{10,11... | collective-permute-start | bytes 1769480 | tf_op jit(solution)/shard_map/ppermute | solution.py:59
  288.3 16.4 %collective-permute-start.44 = (bf16[4,48,384]{2,1,0:T(8,128)(2,1)S(1)}, bf16[4,48,384]{2,1,0:T(8,128)(2,1)S(1)}, u32[]{:S(2)}, u32[]{:S(2)}) collective-permute-start(bf16[4,48,384]{2,1,0:T(8,128)(2,1)S(1)} %pad_maximum_fusion.21), channel_id=1, source_target_pairs={{0,1},{1,0},{2,3},{3,2},{4,5},{5,4},{6,7},{7,6},{8,9},{9,8},{10,11... | collective-permute-start | bytes 442376 | tf_op jit(solution)/shard_map/ppermute | solution.py:59
  334.2 13.7 %collective-permute-start.64 = (f32[96,384]{1,0:T(8,128)S(1)}, f32[96,384]{1,0:T(8,128)S(1)}, u32[]{:S(2)}, u32[]{:S(2)}) collective-permute-start(f32[96,384]{1,0:T(8,128)S(1)} %get-tuple-element.200), channel_id=1, source_target_pairs={{0,16},{8,24},{16,0},{24,8},{1,17},{9,25},{17,1},{25,9},{2,18},{10... | collective-permute-start | bytes 442376 | tf_op jit(solution)/shard_map/ppermute | solution.py:54
  348.8 12.3 %collective-permute-start.67 = (f32[96,384]{1,0:T(8,128)S(1)}, f32[96,384]{1,0:T(8,128)S(1)}, u32[]{:S(2)}, u32[]{:S(2)}) collective-permute-start(f32[96,384]{1,0:T(8,128)S(1)} %fusion.78), channel_id=1, source_target_pairs={{0,16},{8,24},{16,0},{24,8},{1,17},{9,25},{17,1},{25,9},{2,18},{10... | collective-permute-start | bytes 442376 | tf_op jit(solution)/shard_map/ppermute | solution.py:54
  348.8 12.3 %collective-permute-start.66 = (f32[96,384]{1,0:T(8,128)S(1)}, f32[96,384]{1,0:T(8,128)S(1)}, u32[]{:S(2)}, u32[]{:S(2)}) collective-permute-start(f32[96,384]{1,0:T(8,128)S(1)} %fusion.78), channel_id=1, source_target_pairs={{0,8},{8,16},{16,24},{24,0},{1,9},{9,17},{17,25},{25,1},{2,10},{10... | collective-permute-start | bytes 442376 | tf_op jit(solution)/shard_map/ppermute | solution.py:54
  394.0 10.8 %collective-permute-start.70 = (bf16[2,384,288]{1,2,0:T(8,128)(2,1)S(1)}, bf16[2,384,288]{1,2,0:T(8,128)(2,1)S(1)}, u32[]{:S(2)}, u32[]{:S(2)}) collective-permute-start(bf16[2,384,288]{1,2,0:T(8,128)(2,1)S(1)} %pad_maximum_fusion.12), channel_id=1, source_target_pairs={{0,4},{1,5},{2,6},{3,7},{4,0},{5,1},{6,2},{7,3},{8,12},{9,13},{10,... | collective-permute-start | bytes 1327112 | tf_op jit(solution)/shard_map/ppermute | solution.py:59
  396.8 16.6 %collective-permute-start.75 = (f32[1056]{0:T(1024)S(1)}, f32[1056]{0:T(1024)S(1)}, u32[]{:S(2)}, u32[]{:S(2)}) collective-permute-start(f32[1056]{0:T(1024)S(1)} %add_add_fusion), channel_id=1, source_target_pairs={{0,2},{1,3},{2,0},{3,1},{4,6},{5,7},{6,4},{7,5},{8,10},{9,11},{10,... | collective-permute-start | bytes 12680 | tf_op jit(solution)/shard_map/ppermute | solution.py:59
  405.8 19.3 %collective-permute-start.71 = (bf16[4,384,288]{1,2,0:T(8,128)(2,1)}, bf16[4,384,288]{1,2,0:T(8,128)(2,1)}, u32[]{:S(2)}, u32[]{:S(2)}) collective-permute-start(bf16[4,384,288]{1,2,0:T(8,128)(2,1)} %pad_maximum_fusion.5), channel_id=1, source_target_pairs={{0,1},{1,0},{2,3},{3,2},{4,5},{5,4},{6,7},{7,6},{8,9},{9,8},{10,11... | collective-permute-start | bytes 2654216 | tf_op jit(solution)/shard_map/ppermute | solution.py:59
  406.0 13.1 %collective-permute-start.30 = (f32[4,384]{1,0:T(4,128)S(1)}, f32[4,384]{1,0:T(4,128)S(1)}, u32[]{:S(2)}, u32[]{:S(2)}) collective-permute-start(f32[4,384]{1,0:T(4,128)S(1)} %get-tuple-element.217), channel_id=1, source_target_pairs={{0,24},{8,0},{16,8},{24,16},{1,25},{9,1},{17,9},{25,17},{2,26},{10... | collective-permute-start | bytes 18440 | tf_op jit(solution)/shard_map/ppermute | solution.py:54
  (158 other events, 1382.0 us)
